TPU v7x, 512 devices: a whole 4x4x16 slice. The times are simulated.
512 devices in a mesh: depth: 64 (over x, z), rays: 8 (over y, core).
Axes of the slice: x: 4, y: 4, z: 16, core: 2. Of those that a mesh axis runs over, the one named last changes fastest.
Arguments:
- encoded: bfloat16 [64, 4, 4096, 256], P('depth', None, 'rays'), may hold values from -6 to 6
- deltas: float32 [64, 4, 4096], P('depth', None, 'rays'), may hold values from 0.00390625 to 0.03125
- w_in: bfloat16 [64, 256, 512], P('depth'), may hold values from -0.375 to 0.375
- w_mid: bfloat16 [64, 512, 512], P('depth'), may hold values from -0.25 to 0.25
- w_sigma: bfloat16 [64, 512], P('depth'), may hold values from -0.25 to 0.25
- order: int32 [8, 64], P('rays'), may hold values from 0 to 63, each once within a row
- target: bfloat16 [4096, 512], P('rays'), may hold values from -3 to 3
Outputs:
- grad_in: float32 [64, 256, 512], P('depth', 'rays')
- grad_mid: float32 [64, 512, 512], P('depth', 'rays')
- grad_sigma: float32 [64, 512], P('depth', 'rays')
- loss: float32 [], replicated
Inputs may be any that keep to these rules, and one draw needn't show every extreme that they name: Each row of order lists every region once.
All inputs are finite; a program needn't handle non-finite values.
Results may differ from a plain program's by a relative error of at most 0.015.
Values may be sent and summed in bfloat16 or wider, within the bound.
A program may use at most 64 MiB of HBM per device.

v0:
```python
import jax
import jax.numpy as jnp
from jax import lax
from jax.sharding import PartitionSpec as P


def contract_rows(left, right):
    return lax.dot_general(
        left, right, (((0,), (0,)), ((), ())), preferred_element_type=jnp.float32
    )


def body(encoded, deltas, w_in, w_mid, w_sigma, order, target):
    samples = encoded.shape[1]
    rays_dev = encoded.shape[2]
    width_in = encoded.shape[3]
    rows = encoded[0].reshape(samples * rays_dev, width_in)
    first = w_in[0]
    second = w_mid[0]
    density = w_sigma[0]
    spacing = deltas[0]
    hidden = jnp.maximum(jnp.dot(rows, first, preferred_element_type=jnp.float32), 0.0)
    hidden_b = hidden.astype(jnp.bfloat16)
    feat = jnp.dot(hidden_b, second, preferred_element_type=jnp.float32)
    logit = jnp.dot(hidden_b, density, preferred_element_type=jnp.float32)
    features = feat.shape[1]
    tau = jax.nn.softplus(logit).reshape(samples, rays_dev) * spacing
    excl = jnp.cumsum(tau, axis=0) - tau
    weight = jnp.exp(-excl) * (1.0 - jnp.exp(-tau))
    feat3 = feat.reshape(samples, rays_dev, features)
    segment = jnp.sum(weight[:, :, None] * feat3, axis=0)
    depth_tau = jnp.sum(tau, axis=0)
    regions = lax.axis_size("depth")
    region_me = lax.axis_index("depth")
    positions = jnp.arange(regions, dtype=jnp.int32)
    onehot = order[0][:, None] == positions[None, :]
    rank = jnp.sum(jnp.where(onehot, positions[:, None], 0), axis=0)
    rank_me = jnp.sum(jnp.where(positions == region_me, rank, 0))
    before = (rank < rank_me).astype(jnp.float32)
    after = (rank > rank_me).astype(jnp.float32)
    all_tau = lax.all_gather(depth_tau[None], "depth", axis=0, tiled=True)
    prefix = jnp.dot(before, all_tau, precision=lax.Precision.HIGHEST)
    trans = jnp.exp(-prefix)
    weighted = trans[:, None] * segment
    count_total = rays_dev * lax.axis_size("rays") * features
    color = lax.psum(weighted, "depth")
    err = color - target.astype(jnp.float32)
    loss = lax.psum(jnp.sum(err * err), "rays") / count_total
    dcolor = lax.optimization_barrier(err.astype(jnp.bfloat16)).astype(jnp.float32)
    qsum = jnp.sum(segment * dcolor, axis=1)
    all_terms = lax.all_gather((trans * qsum)[None], "depth", axis=0, tiled=True)
    gtau = -jnp.dot(after, all_terms, precision=lax.Precision.HIGHEST)
    dseg = trans[:, None] * dcolor
    dfeat = (weight[:, :, None] * dseg[None]).astype(jnp.bfloat16)
    vsum = jnp.sum(feat3 * dseg[None], axis=2)
    wv = weight * vsum
    dtau = (
        jnp.exp(-(excl + tau)) * vsum
        - (jnp.sum(wv, axis=0)[None] - jnp.cumsum(wv, axis=0))
        + gtau[None]
    )
    dz = (dtau * spacing).reshape(-1) * jax.nn.sigmoid(logit)
    dfeat2 = dfeat.reshape(samples * rays_dev, features)
    part_mid = contract_rows(hidden_b, dfeat2)
    part_sig = jnp.sum(hidden_b * dz[:, None], axis=0)
    dhb = lax.dot_general(
        dfeat2, second, (((1,), (1,)), ((), ())), preferred_element_type=jnp.float32
    )
    dhb = dhb + dz[:, None] * density.astype(jnp.float32)[None]
    dpre = jnp.where(hidden > 0, dhb, 0.0).astype(jnp.bfloat16)
    part_in = contract_rows(rows, dpre)
    grad_in, grad_mid, grad_sigma = (
        lax.psum_scatter(
            part_in.astype(jnp.bfloat16), "rays", scatter_dimension=0, tiled=True
        ).astype(jnp.float32),
        lax.psum_scatter(
            part_mid.astype(jnp.bfloat16), "rays", scatter_dimension=0, tiled=True
        ).astype(jnp.float32),
        lax.psum_scatter(
            part_sig.astype(jnp.bfloat16), "rays", scatter_dimension=0, tiled=True
        ).astype(jnp.float32),
    )
    return (grad_in[None], grad_mid[None], grad_sigma[None], loss)


def solution(mesh):
    in_specs = (
        P("depth", None, "rays", None),
        P("depth", None, "rays"),
        P("depth", None, None),
        P("depth", None, None),
        P("depth", None),
        P("rays", None),
        P("rays", None),
    )
    out_specs = (P("depth", "rays", None), P("depth", "rays", None), P("depth", "rays"), P())
    return jax.shard_map(body, mesh=mesh, in_specs=in_specs, out_specs=out_specs, check_vma=False)
```

profile of v0, /device:TPU:2, one launch (start us, length us, event | category | flops | bytes accessed | tf_op | source)
XLA Modules:
  0.0 594.7 jit_solution(4081673140898898454)
XLA Ops:
  7.2 1.2 copy-done
  8.4 3.6 maximum_convert_fusion
  12.0 0.6 fusion.16
  12.8 105.5 %all-gather.2 = f32[64,1,512]{2,1,0:T(1,128)S(1)} all-gather(f32[1,1,512]{2,1,0:T(1,128)S(1)} %bitcast.96), channel_id=2, replica_groups=mesh['depth'=64,'rays'=8] {'depth'}, dimensions={0}, use_global_device_ids=true | all-gather | bytes 133120 | tf_op jit(solution)/shard_map/all_gather | solution.py:41
  118.3 0.1 select_reduce_fusion
  118.4 0.6 fusion.22
  119.0 0.8 fusion.13
  119.9 4.5 multiply_reduce_fusion.2
  124.4 1.1 copy-done.2
  125.4 1.1 broadcast_multiply_fusion
  126.6 2.0 copy.25
  128.7 266.2 %all-reduce.3.cloned.1.call-done = f32[512,512]{0,1:T(8,128)} async-done(((f32[512,512]{0,1:T(8,128)}), f32[512,512]{0,1:T(8,128)}) %all-reduce.3.cloned.1.call-update) | async-done | bytes 1048592 | tf_op jit(solution)/shard_map/psum | solution.py:46
  394.9 2.4 multiply_reduce_fusion.3
  397.3 1.4 fusion.2
  398.8 2.2 multiply_reduce_fusion.1
  400.9 4.1 copy.26
  405.1 97.8 %all-gather.3 = f32[64,1,512]{2,1,0:T(1,128)S(1)} all-gather(f32[1,1,512]{2,1,0:T(1,128)S(1)} %bitcast.94), channel_id=3, replica_groups=mesh['depth'=64,'rays'=8] {'depth'}, dimensions={0}, use_global_device_ids=true | all-gather | bytes 133120 | tf_op jit(solution)/shard_map/all_gather | solution.py:51
  502.8 0.8 fusion.10
  503.8 5.7 fusion.1
  509.5 0.9 copy.31
  510.4 2.6 copy.35
  513.0 1.6 fusion
  514.6 2.1 convolution_convert_fusion
  516.7 1.3 dynamic-slice
  518.6 13.1 %psum.15 = f32[]{:T(128)} all-reduce(f32[]{:T(128)} %get-tuple-element.24), channel_id=1, replica_groups=mesh['depth'=64,'rays'=8] {'rays'}, use_global_device_ids=true, to_apply=%region_15.16 | all-reduce | flops 1 | bytes 8 | tf_op jit(solution)/shard_map/psum | solution.py:48
  532.3 0.5 multiply_reduce_fusion
  532.8 12.5 %all-reduce = bf16[512]{0:T(512)(128)(2,1)S(1)} all-reduce(bf16[512]{0:T(512)(128)(2,1)S(1)} %multiply_reduce_fusion), channel_id=6, replica_groups=mesh['depth'=64,'rays'=8] {'rays'}, use_global_device_ids=true, to_apply=%region_13.14.clone | all-reduce | flops 512 | bytes 2048
  545.2 0.6 bitcast_convert_fusion.2
  545.8 0.9 copy.32
  546.7 0.7 copy.28
  547.5 38.0 %reduce-scatter.5.cloned.1.call-done = bf16[64,512]{1,0:T(8,128)(2,1)} async-done(((bf16[512,512]{1,0:T(8,128)(2,1)}), bf16[64,512]{1,0:T(8,128)(2,1)}) %reduce-scatter.5.cloned.1.call-update) | async-done | bytes 65552 | tf_op jit(solution)/shard_map/reduce_scatter | solution.py:76
  585.5 1.5 bitcast_convert_fusion.1
  (40 shorter events, 0.5 us)
Async XLA Ops:
  7.2 1.2 copy-start
  7.2 4.8 copy-start.5
  7.2 387.7 %all-reduce.3.cloned.1.call-start = ((), (), s32[]{:S(2)}) async-start(), calls=%async_computation.2 | async-start | bytes 2097152 | tf_op jit(solution)/shard_map/psum | solution.py:46
  8.4 4.3 copy-start.4
  8.4 109.9 %copy-start.6 = (s32[1,64]{1,0:T(1,128)S(1)}, s32[1,64]{1,0:T(1,128)}, u32[]{:S(2)}) copy-start(s32[1,64]{1,0:T(1,128)} %param.12) | copy-start | bytes 772
  124.4 1.1 copy-start.2
  126.6 419.3 %reduce-scatter.7.cloned.1.call-start = ((), (), s32[]{:S(2)}) async-start(), calls=%async_computation.4 | async-start | bytes 294912
  394.9 3.8 copy-start.1
  398.8 2.2 copy-start.3
  510.4 75.1 %reduce-scatter.5.cloned.1.call-start = ((), (), s32[]{:S(2)}) async-start(), calls=%async_computation.3 | async-start | bytes 589824 | tf_op jit(solution)/shard_map/reduce_scatter | solution.py:76
Sparse Core Ops, SparseCore 0:
  126.7 268.2 all-reduce.2
  510.5 34.6 reduce-scatter.6
  548.0 37.4 reduce-scatter.4
where the time goes:
time: 595 us
  waiting for transfers between devices  304 us (51%)
  blocking collectives  229 us (38%)
  matrix products  18.1 us (3%)
  between operations  16.3 us (3%)
  local copies, waits for them, and re-layouts  14.8 us (2%)
  other arithmetic  12.2 us (2%)
    psum x1, waiting for transfers between devices, body(): color = lax.psum(weighted, 'depth')  266 us
    all_gather x1, blocking collectives, body(): all_tau = lax.all_gather(depth_tau[None], 'depth', axis=0, tiled=True)  106 us
    all_gather x1, blocking collectives, body(): lax.all_gather((trans * qsum)[None], 'depth', axis=0, tiled=True)  97.8 us
    reduce_scatter x1, waiting for transfers between devices, body(): lax.psum_scatter(part_mid.astype(jnp.bfloat16), 'rays', scatter_dimension...  38 us
    psum x1, blocking collectives, body(): loss = lax.psum(jnp.sum(err * err), 'rays') / count_total  13.1 us
    unnamed x1, blocking collectives  12.5 us
  transfers between devices with their start and end apart: 3, of which 2 were waited for; matrix products, arithmetic and copies ran while one was open for 2% of the time, Pallas kernels for 0%

commit v1 on v0

--- a/solution.py
+++ b/solution.py
@@ -48,7 +48,10 @@
     loss = lax.psum(jnp.sum(err * err), "rays") / count_total
     dcolor = lax.optimization_barrier(err.astype(jnp.bfloat16)).astype(jnp.float32)
     qsum = jnp.sum(segment * dcolor, axis=1)
-    all_terms = lax.all_gather((trans * qsum)[None], "depth", axis=0, tiled=True)
+    all_terms = jnp.concatenate(
+        lax.all_to_all(jnp.stack([(trans * qsum)[None]] * lax.axis_size("depth")), "depth", 0, 0),
+        axis=0,
+    )
     gtau = -jnp.dot(after, all_terms, precision=lax.Precision.HIGHEST)
     dseg = trans[:, None] * dcolor
     dfeat = (weight[:, :, None] * dseg[None]).astype(jnp.bfloat16)

time: 595 us -> 516 us (0.87)
  blocking collectives: 229 us -> 131 us
  starting transfers between devices: 0.12 us -> 10.3 us
    all_gather x1 -> x0, blocking collectives: 97.8 us -> none  [body(): lax.all_gather((trans * qsum)[None], 'depth', axis=0, tiled=True)]
    all_to_all x0 -> x1, starting transfers between devices: none -> 10.1 us  [body(): lax.all_to_all(jnp.stack([(trans * qsum)[None]] * lax.axis_size('depth'))...]
  transfers between devices with their start and end apart: 3 -> 4, of which waited for: 2 -> 3; matrix products, arithmetic and copies ran while one was open for 2% -> 4% of each run, Pallas kernels for 0% -> 0%
where the time goes in v1:
time: 516 us
  waiting for transfers between devices  309 us (60%)
  blocking collectives  131 us (25%)
  matrix products  18.1 us (4%)
  between operations  16.3 us (3%)
  local copies, waits for them, and re-layouts  15.5 us (3%)
  other arithmetic  15.5 us (3%)
  starting transfers between devices  10.3 us (2%)
    psum x1, waiting for transfers between devices, body(): color = lax.psum(weighted, 'depth')  266 us
    all_gather x1, blocking collectives, body(): all_tau = lax.all_gather(depth_tau[None], 'depth', axis=0, tiled=True)  106 us
    reduce_scatter x1, waiting for transfers between devices, body(): lax.psum_scatter(part_mid.astype(jnp.bfloat16), 'rays', scatter_dimension...  37.1 us
    psum x1, blocking collectives, body(): loss = lax.psum(jnp.sum(err * err), 'rays') / count_total  13.1 us
    unnamed x1, blocking collectives  12.4 us
    unnamed x22, local copies, waits for them, and re-layouts  10.6 us
  transfers between devices with their start and end apart: 4, of which 3 were waited for; matrix products, arithmetic and copies ran while one was open for 4% of the time, Pallas kernels for 0%

profile of v1, /device:TPU:2, one launch (start us, length us, event | category | flops | bytes accessed | tf_op | source)
XLA Modules:
  0.0 515.5 jit_solution(17797704551915750924)
XLA Ops:
  7.2 1.2 copy-done
  8.4 3.6 maximum_convert_fusion
  12.0 0.6 fusion.16
  12.8 105.5 %all-gather.1 = f32[64,1,512]{2,1,0:T(1,128)S(1)} all-gather(f32[1,1,512]{2,1,0:T(1,128)S(1)} %bitcast.94), channel_id=2, replica_groups=mesh['depth'=64,'rays'=8] {'depth'}, dimensions={0}, use_global_device_ids=true | all-gather | bytes 133120 | tf_op jit(solution)/shard_map/all_gather | solution.py:41
  118.4 0.6 fusion.22
  119.0 0.8 fusion.13
  119.9 4.5 multiply_reduce_fusion.2
  124.4 1.1 copy-done.1
  125.4 1.1 broadcast_multiply_fusion
  126.6 2.0 copy.25
  128.7 266.3 %all-reduce.3.cloned.1.call-done = f32[512,512]{0,1:T(8,128)} async-done(((f32[512,512]{0,1:T(8,128)}), f32[512,512]{0,1:T(8,128)}) %all-reduce.3.cloned.1.call-update) | async-done | bytes 1048592 | tf_op jit(solution)/shard_map/psum | solution.py:46
  394.9 2.2 multiply_reduce_fusion.3
  397.2 2.4 fusion.2
  399.6 0.7 stack.3
  400.3 10.1 %all-to-all-start = ((f32[64,1,512]{2,1,0:T(1,128)}), f32[64,1,512]{2,1,0:T(1,128)S(1)}, u32[]{:S(2)}, u32[]{:S(2)}) async-start(f32[64,1,512]{2,1,0:T(1,128)} %stack.3), calls=%async_computation | async-start | bytes 262144 | tf_op jit(solution)/shard_map/all_to_all | solution.py:52
  410.5 4.6 multiply_reduce_fusion.1
  415.1 4.1 copy.26
  419.3 5.3 %all-to-all-done = f32[64,1,512]{2,1,0:T(1,128)S(1)} async-done(((f32[64,1,512]{2,1,0:T(1,128)}), f32[64,1,512]{2,1,0:T(1,128)S(1)}, u32[]{:S(2)}, u32[]{:S(2)}) %all-to-all-start) | async-done | bytes 131104 | tf_op jit(solution)/shard_map/all_to_all | solution.py:52
  424.6 0.8 fusion.10
  425.5 5.7 %fusion.1 = bf16[256,512]{0,1:T(8,128)(2,1)S(1)} fusion(bf16[2048,256]{1,0:T(8,128)(2,1)S(1)} %bitcast.78, f32[2048,512]{1,0:T(8,128)} %get-tuple-element.33, bf16[2048,512]{1,0:T(8,128)(2,1)} %bitcast.80, f32[512]{0:T(512)S(1)} %mul.137, f32[2048]{0:T(1024)S(1)} %get-tuple-element.31, bf16[1,512,512]{2,1,0:T(8,128)(2,1)} %param.10), kind=kOutput, calls=%fused_computation.12 | convolution fusion | flops 1615986688 | bytes 8136704 | tf_op jit(solution)/shard_map/dot_general | solution.py:8
  431.2 0.9 copy.31
  432.2 2.6 copy.35
  434.7 1.6 fusion
  436.3 2.1 convolution_convert_fusion
  438.4 1.3 dynamic-slice
  440.3 13.1 %psum.15 = f32[]{:T(128)} all-reduce(f32[]{:T(128)} %get-tuple-element.24), channel_id=1, replica_groups=mesh['depth'=64,'rays'=8] {'rays'}, use_global_device_ids=true, to_apply=%region_15.16 | all-reduce | flops 1 | bytes 8 | tf_op jit(solution)/shard_map/psum | solution.py:48
  454.5 12.4 %all-reduce = bf16[512]{0:T(512)(128)(2,1)S(1)} all-reduce(bf16[512]{0:T(512)(128)(2,1)S(1)} %multiply_reduce_fusion), channel_id=5, replica_groups=mesh['depth'=64,'rays'=8] {'rays'}, use_global_device_ids=true, to_apply=%region_13.14.clone | all-reduce | flops 512 | bytes 2048
  467.0 0.6 bitcast_convert_fusion.2
  467.5 0.9 copy.32
  468.5 0.7 copy.28
  469.2 37.1 %reduce-scatter.5.cloned.1.call-done = bf16[64,512]{1,0:T(8,128)(2,1)} async-done(((bf16[512,512]{1,0:T(8,128)(2,1)}), bf16[64,512]{1,0:T(8,128)(2,1)}) %reduce-scatter.5.cloned.1.call-update) | async-done | bytes 65552 | tf_op jit(solution)/shard_map/reduce_scatter | solution.py:79
  506.3 1.5 bitcast_convert_fusion.1
  (38 shorter events, 1.1 us)
Async XLA Ops:
  7.2 1.2 copy-start
  7.2 4.8 copy-start.3
  7.2 387.7 %all-reduce.3.cloned.1.call-start = ((), (), s32[]{:S(2)}) async-start(), calls=%async_computation.3 | async-start | bytes 2097152 | tf_op jit(solution)/shard_map/psum | solution.py:46
  8.4 4.3 copy-start.2
  8.4 109.9 %copy-start.4 = (s32[1,64]{1,0:T(1,128)S(1)}, s32[1,64]{1,0:T(1,128)}, u32[]{:S(2)}) copy-start(s32[1,64]{1,0:T(1,128)} %param.12) | copy-start | bytes 772
  124.4 1.1 copy-start.1
  400.3 24.3 %all-to-all-start = ((f32[64,1,512]{2,1,0:T(1,128)}), f32[64,1,512]{2,1,0:T(1,128)S(1)}, u32[]{:S(2)}, u32[]{:S(2)}) async-start(f32[64,1,512]{2,1,0:T(1,128)} %stack.3), calls=%async_computation | async-start | bytes 262144 | tf_op jit(solution)/shard_map/all_to_all | solution.py:52
  410.4 57.1 %reduce-scatter.7.cloned.1.call-start = ((), (), s32[]{:S(2)}) async-start(), calls=%async_computation.5 | async-start | bytes 294912
  432.1 74.2 %reduce-scatter.5.cloned.1.call-start = ((), (), s32[]{:S(2)}) async-start(), calls=%async_computation.4 | async-start | bytes 589824 | tf_op jit(solution)/shard_map/reduce_scatter | solution.py:79
Sparse Core Ops, SparseCore 0:
  126.7 268.2 all-reduce.2
  432.2 33.6 reduce-scatter.6
  468.8 37.5 reduce-scatter.4
